TPU v7x, 32 devices: a whole 2x2x4 slice. The times are simulated.
32 devices in a mesh: groups: 2 (over x), loop: 8 (over z, y), narrow: 2 (over core).
Axes of the slice: x: 2, y: 2, z: 4, core: 2. Of those that a mesh axis runs over, the one named last changes fastest.
Arguments:
- src_points: bfloat16 [512, 64, 128], P(('groups', 'loop', 'narrow')), parts along dimension 0
- tgt_points: bfloat16 [128, 64, 128], P(('groups', 'loop')), parts along dimension 0
- block_list: int32 [512, 24], P(('groups', 'loop', 'narrow')), parts along dimension 0, may hold values from 0 to 63, as said below
- list_len: int32 [512], P(('groups', 'loop', 'narrow')), parts along dimension 0, may hold values from 1 to 24
- src_counts: int32 [512], P(('groups', 'loop', 'narrow')), parts along dimension 0, may hold values from 1 to 128
- tgt_counts: int32 [128], P(('groups', 'loop')), parts along dimension 0, may hold values from 1 to 128
Outputs:
- src_field: float32 [512, 128], P(('groups', 'loop', 'narrow')), parts along dimension 0
- tgt_field: float32 [128, 128], P(('groups', 'loop')), parts along dimension 0
There are 2 independent parts, one for each index of `groups`. A program takes and returns all parts, laid end to end along the dimension named above; each array names one. Nothing has to cross between parts.
Inputs may be any that keep to these rules, and one draw needn't show every extreme that they name: `block_list`: every entry of row i names a target block whose loop position t // 8 lies within 3 positions, cyclically over the loop's 8 positions, of the source block's loop position i // 32; only the first list_len[i] entries are used; every target block is named by a used entry of some source block.
All inputs are finite; a program needn't handle non-finite values.
Results may differ from a plain program's by a relative error of at most 0.0003.
Values may be sent and summed in bfloat16 or wider, within the bound.
A program may use at most 64 MiB of HBM per device.

v0:
```python
import jax
import jax.numpy as jnp
from jax import lax
from jax.sharding import PartitionSpec as P

REACH = 3
ITERS = 2


EPSILON = 0.05
FILL_VALUE = -1e30


def passed_along(block, axis, distance):
    devices = range(lax.axis_size(axis))
    route = [((i - distance) % len(devices), i) for i in devices]
    return lax.ppermute(block, axis, route)


def merged(value, axis, join):
    pieces = lax.all_gather(value, axis)
    head = pieces[0]
    tail = pieces[1:]
    running, _ = lax.scan(lambda running, slab: (join(running, slab), None), head, tail)
    return running


def lse_join(first, second):
    highest = jnp.maximum(first, second)
    return highest + jnp.log(jnp.exp(first - highest) + jnp.exp(second - highest))


def block_cost(source, source_sq, targets, target_sq):
    cross = jnp.einsum("dr,kdc->krc", source, targets, preferred_element_type=jnp.float32)
    return source_sq[None, :, None] + target_sq[:, None, :] - 2.0 * cross


def local(src_points, tgt_points, block_list, list_len, src_counts, tgt_counts):
    loop_size = lax.axis_size("loop")
    loop_index = lax.axis_index("loop")
    tgt_blocks = tgt_points.shape[0]
    feat_count = tgt_points.shape[1]
    block_rows = tgt_points.shape[2]
    src_blocks = src_points.shape[0]
    list_slots = block_list.shape[1]
    window_blocks = (2 * REACH + 1) * tgt_blocks
    row_iota = jnp.arange(block_rows)
    src_valid = row_iota[None, :] < src_counts[:, None]
    tgt_valid = row_iota[None, :] < tgt_counts[:, None]
    slot_live = jnp.arange(list_slots)[None, :] < list_len[:, None]
    home_group = jnp.mod(block_list // tgt_blocks - loop_index + REACH, loop_size)
    window_index = jnp.clip(home_group * tgt_blocks + block_list % tgt_blocks, 0, window_blocks - 1)
    slot_pick = window_index[:, :, None] == jnp.arange(window_blocks)[None, None, :]
    flat_pick = slot_pick.reshape(-1, window_blocks)
    choose = flat_pick.T.astype(jnp.float32)
    src_squares = jnp.sum(jnp.square(src_points.astype(jnp.float32)), axis=1)
    placed = {0: tgt_points}
    for offset in range(-REACH, REACH + 1):
        if offset != 0:
            placed[offset] = passed_along(tgt_points, "loop", -offset)
    window_points = jnp.concatenate([placed[offset] for offset in range(-REACH, REACH + 1)], axis=0)
    window_flat = window_points.reshape(window_blocks, feat_count * block_rows)
    chosen = jnp.einsum(
        "skw,wx->skx",
        slot_pick.astype(jnp.bfloat16),
        window_flat,
        preferred_element_type=jnp.float32,
    )
    chosen = chosen.astype(jnp.bfloat16).reshape(src_blocks, list_slots, feat_count, block_rows)
    chosen_sq = jnp.sum(jnp.square(chosen.astype(jnp.float32)), axis=2)

    def spread_potential(masked):
        held = {0: masked}
        for offset in range(-REACH, REACH + 1):
            if offset != 0:
                held[offset] = passed_along(masked, "loop", -offset)
        return jnp.concatenate([held[offset] for offset in range(-REACH, REACH + 1)], axis=0)

    tgt_field = jnp.zeros((tgt_blocks, block_rows), jnp.float32)
    src_field = jnp.zeros((src_blocks, block_rows), jnp.float32)
    for iteration in range(ITERS):
        window_potential = spread_potential(jnp.where(tgt_valid, tgt_field, FILL_VALUE))
        picked_potential = jnp.sum(
            jnp.where(slot_pick[:, :, :, None], window_potential[None, None, :, :], 0.0), axis=2
        )

        def row_block(inputs):
            source, source_sq, targets, target_sq, potential, slot_ok, row_ok = inputs
            pair_cost = block_cost(source, source_sq, targets, target_sq)
            allowed = slot_ok[:, None, None] & (potential > 0.5 * FILL_VALUE)[:, None, :]
            scores = jnp.where(allowed, (potential[:, None, :] - pair_cost) / EPSILON, FILL_VALUE)
            row_peak = jnp.max(scores, axis=(0, 2))
            summed = jnp.sum(
                jnp.where(allowed, jnp.exp(scores - row_peak[None, :, None]), 0.0), axis=(0, 2)
            )
            return jnp.where(row_ok, -EPSILON * (row_peak + jnp.log(summed)), 0.0)

        src_field = lax.map(
            row_block,
            (src_points, src_squares, chosen, chosen_sq, picked_potential, slot_live, src_valid),
        )

        def column_block(inputs):
            source, source_sq, targets, target_sq, slot_ok, row_field, row_ok = inputs
            pair_cost = block_cost(source, source_sq, targets, target_sq)
            allowed = row_ok[None, :, None]
            scores = jnp.where(
                allowed, (row_field[None, :, None] - pair_cost) / EPSILON, FILL_VALUE
            )
            col_peak = jnp.max(scores, axis=1)
            summed = jnp.sum(
                jnp.where(allowed, jnp.exp(scores - col_peak[:, None, :]), 0.0), axis=1
            )
            return jnp.where(slot_ok[:, None], col_peak + jnp.log(summed), FILL_VALUE)

        partial_value = lax.map(
            column_block,
            (src_points, src_squares, chosen, chosen_sq, slot_live, src_field, src_valid),
        )
        partial_value = partial_value.reshape(-1, block_rows)
        window_peak = jnp.max(
            jnp.where(flat_pick.T[:, :, None], partial_value[None, :, :], FILL_VALUE), axis=1
        )
        peak_back = jnp.sum(jnp.where(flat_pick[:, :, None], window_peak[None, :, :], 0.0), axis=1)
        window_sum = jnp.dot(
            choose, jnp.exp(partial_value - peak_back), precision=lax.Precision.HIGHEST
        )
        window_lse = window_peak + jnp.log(jnp.where(window_sum > 0.0, window_sum, 1.0))

        def group_at(offset):
            return window_lse[(offset + REACH) * tgt_blocks : (offset + REACH + 1) * tgt_blocks]

        column_lse = group_at(0)
        for offset in range(-REACH, REACH + 1):
            if offset != 0:
                column_lse = lse_join(column_lse, passed_along(group_at(offset), "loop", offset))
        column_lse = merged(column_lse, "narrow", lse_join)
        tgt_field = jnp.where(tgt_valid, -EPSILON * column_lse, 0.0)
    return (src_field, tgt_field)


def solution(mesh):
    placed = (
        P(("groups", "loop", "narrow"), None, None),
        P(("groups", "loop"), None, None),
        P(("groups", "loop", "narrow"), None),
        P(("groups", "loop", "narrow")),
        P(("groups", "loop", "narrow")),
        P(("groups", "loop")),
    )
    return jax.shard_map(
        local,
        mesh=mesh,
        in_specs=placed,
        out_specs=(P(("groups", "loop", "narrow"), None), P(("groups", "loop"), None)),
        check_vma=False,
    )
```

profile of v0, /device:TPU:0, one launch (start us, length us, event | category | flops | bytes accessed | tf_op | source)
XLA Modules:
  0.0 326.4 jit_solution(10534852467942536626)
XLA Ops:
  1.4 4.0 %collective-permute-start = (f32[8,128]{1,0:T(8,128)S(1)}, f32[8,128]{1,0:T(8,128)S(1)}, u32[]{:S(2)}, u32[]{:S(2)}) collective-permute-start(f32[8,128]{1,0:T(8,128)S(1)} %fusion.89), channel_id=1, source_target_pairs={{10,0},{12,2},{14,4},{0,6},{2,8},{4,10},{6,12},{8,14},{11,1},{13,3... | collective-permute-start | bytes 12296 | tf_op jit(solution)/shard_map/ppermute | solution.py:17
  8.5 3.2 collective-permute-start.3
  21.0 4.7 %collective-permute-start.9 = (bf16[8,64,128]{2,1,0:T(8,128)(2,1)}, bf16[8,64,128]{2,1,0:T(8,128)(2,1)S(1)}, u32[]{:S(2)}, u32[]{:S(2)}) collective-permute-start(bf16[8,64,128]{2,1,0:T(8,128)(2,1)} %param.15), channel_id=1, source_target_pairs={{2,0},{4,2},{6,4},{8,6},{10,8},{12,10},{14,12},{0,14},{3,1},{5,3},... | collective-permute-start | bytes 393224 | tf_op jit(solution)/shard_map/ppermute | solution.py:17
  26.2 4.9 %select_reduce_fusion.9 = f32[16,24,128]{2,1,0:T(8,128)S(1)} fusion(f32[56,128]{1,0:T(8,128)S(1)} %constant_dynamic-update-slice_fusion, pred[16,24,56]{2,1,0:T(8,128)(4,1)S(1)} %iota_compare_fusion.1), kind=kLoop, calls=%fused_computation.83 | loop fusion | flops 5455872 | bytes 246784 | tf_op jit(solution)/shard_map/reduce_sum | solution.py:83
  31.4 5.9 %collective-permute-done.11 = bf16[8,64,128]{2,1,0:T(8,128)(2,1)S(1)} collective-permute-done((bf16[8,64,128]{2,1,0:T(8,128)(2,1)}, bf16[8,64,128]{2,1,0:T(8,128)(2,1)S(1)}, u32[]{:S(2)}, u32[]{:S(2)}) %collective-permute-start.11) | collective-permute-done | bytes 131104 | tf_op jit(solution)/shard_map/ppermute | solution.py:17
  44.5 64.0 %while.48 = (s32[]{:T(128)}, f32[16,128]{1,0:T(8,128)S(1)}, pred[16,128]{1,0:T(8,128)(4,1)S(1)}, pred[16,24]{1,0:T(8,128)(4,1)S(1)}, f32[16,24,128]{2,1,0:T(8,12...) while((s32[]{:T(128)}, f32[16,128]{1,0:T(8,128)S(1)}, ...), condition=%wide.region_6.7_spmd, body=%wide.region_3.6_spmd.sunk | while | flops 54270080 | bytes 3645261 | solution.py:98
  48.6 3.2 fusion.112
  52.6 3.2 fusion.112
  64.6 3.2 fusion.112
  72.6 3.2 fusion.112
  76.6 3.2 fusion.112
  108.5 33.1 %while.49 = (s32[]{:T(128)}, f32[16,24,128]{2,1,0:T(8,128)S(1)}, pred[16,24]{1,0:T(8,128)(4,1)S(1)}, pred[16,128]{1,0:T(8,128)(4,1)S(1)}, f32[16,128]{1,0:T(8,12...) while((s32[]{:T(128)}, f32[16,24,128]{2,1,0:T(8,128)S(1)}, ...), condition=%wide.region_10.11_spmd, body=%wide.region_7.10_spmd.sunk | while | flops 54263808 | bytes 3671209 | solution.py:116
  141.6 4.6 %select_reduce_fusion.8 = f32[56,128]{1,0:T(8,128)S(1)} fusion(f32[384,128]{1,0:T(8,128)S(1)} %bitcast.192, pred[56,384]{1,0:T(8,128)(4,1)S(1)} %iota_compare_fusion.16), kind=kLoop, calls=%fused_computation.82 | loop fusion | flops 5497856 | bytes 246784 | tf_op jit(solution)/shard_map/reduce_max | solution.py:121
  146.1 14.8 %select_reduce_fusion.7 = f32[384,128]{1,0:T(8,128)S(1)} fusion(f32[56,128]{1,0:T(8,128)S(1)} %select_reduce_fusion.8, pred[384,56]{1,0:T(8,128)(4,1)S(1)} %iota_compare_fusion), kind=kLoop, calls=%fused_computation.81 | loop fusion | flops 5455872 | bytes 246784 | tf_op jit(solution)/shard_map/reduce_sum | solution.py:124
  169.5 3.6 %collective-permute-done.15 = f32[8,128]{1,0:T(8,128)S(1)} collective-permute-done((f32[8,128]{1,0:T(8,128)S(1)}, f32[8,128]{1,0:T(8,128)S(1)}, u32[]{:S(2)}, u32[]{:S(2)}) %collective-permute-start.15) | collective-permute-done | bytes 4128 | tf_op jit(solution)/shard_map/ppermute | solution.py:17
  180.2 3.8 %collective-permute-start.21 = (f32[8,128]{1,0:T(8,128)S(1)}, f32[8,128]{1,0:T(8,128)S(1)}, u32[]{:S(2)}, u32[]{:S(2)}) collective-permute-start(f32[8,128]{1,0:T(8,128)S(1)} %select_select_fusion), channel_id=1, source_target_pairs={{2,0},{4,2},{6,4},{8,6},{10,8},{12,10},{14,12},{0,14},{3,1},{5,3},... | collective-permute-start | bytes 12296 | tf_op jit(solution)/shard_map/ppermute | solution.py:17
  189.2 4.9 %select_reduce_fusion.6 = f32[16,24,128]{2,1,0:T(8,128)S(1)} fusion(f32[56,128]{1,0:T(8,128)S(1)} %constant_dynamic-update-slice_fusion.14, pred[16,24,56]{2,1,0:T(8,128)(4,1)S(1)} %iota_compare_fusion.1), kind=kLoop, calls=%fused_computation.80 | loop fusion | flops 5455872 | bytes 246784 | tf_op jit(solution)/shard_map/reduce_sum | solution.py:83
  194.2 64.0 %while.50 = (s32[]{:T(128)}, f32[16,128]{1,0:T(8,128)S(1)}, pred[16,128]{1,0:T(8,128)(4,1)S(1)}, pred[16,24]{1,0:T(8,128)(4,1)S(1)}, f32[16,24,128]{2,1,0:T(8,12...) while((s32[]{:T(128)}, f32[16,128]{1,0:T(8,128)S(1)}, ...), condition=%wide.region_17.18_spmd, body=%wide.region_14.17_spmd.sunk | while | flops 54270080 | bytes 3645261 | solution.py:98
  194.3 3.2 fusion.119
  198.3 3.2 fusion.119
  202.3 3.2 fusion.119
  258.2 33.1 %while.51 = (s32[]{:T(128)}, f32[16,24,128]{2,1,0:T(8,128)S(1)}, pred[16,24]{1,0:T(8,128)(4,1)S(1)}, pred[16,128]{1,0:T(8,128)(4,1)S(1)}, f32[16,128]{1,0:T(8,12...) while((s32[]{:T(128)}, f32[16,24,128]{2,1,0:T(8,128)S(1)}, ...), condition=%wide.region_21.22_spmd, body=%wide.region_18.21_spmd.sunk | while | flops 54263808 | bytes 3671209 | solution.py:116
  291.3 4.6 %select_reduce_fusion.5 = f32[56,128]{1,0:T(8,128)S(1)} fusion(f32[384,128]{1,0:T(8,128)S(1)} %bitcast.190, pred[56,384]{1,0:T(8,128)(4,1)S(1)} %iota_compare_fusion.16), kind=kLoop, calls=%fused_computation.79 | loop fusion | flops 5497856 | bytes 246784 | tf_op jit(solution)/shard_map/reduce_max | solution.py:121
  295.9 14.8 %select_reduce_fusion.4 = f32[384,128]{1,0:T(8,128)S(1)} fusion(f32[56,128]{1,0:T(8,128)S(1)} %select_reduce_fusion.5, pred[384,56]{1,0:T(8,128)(4,1)S(1)} %iota_compare_fusion), kind=kLoop, calls=%fused_computation.78 | loop fusion | flops 5455872 | bytes 246784 | tf_op jit(solution)/shard_map/reduce_sum | solution.py:124
  (582 shorter events, 223.6 us)
Async XLA Ops:
  1.4 14.3 %collective-permute-start = (f32[8,128]{1,0:T(8,128)S(1)}, f32[8,128]{1,0:T(8,128)S(1)}, u32[]{:S(2)}, u32[]{:S(2)}) collective-permute-start(f32[8,128]{1,0:T(8,128)S(1)} %fusion.89), channel_id=1, source_target_pairs={{10,0},{12,2},{14,4},{0,6},{2,8},{4,10},{6,12},{8,14},{11,1},{13,3... | collective-permute-start | bytes 12296 | tf_op jit(solution)/shard_map/ppermute | solution.py:17
  5.4 10.4 %collective-permute-start.1 = (f32[8,128]{1,0:T(8,128)S(1)}, f32[8,128]{1,0:T(8,128)S(1)}, u32[]{:S(2)}, u32[]{:S(2)}) collective-permute-start(f32[8,128]{1,0:T(8,128)S(1)} %fusion.89), channel_id=1, source_target_pairs={{12,0},{14,2},{0,4},{2,6},{4,8},{6,10},{8,12},{10,14},{13,1},{15,3... | collective-permute-start | bytes 12296 | tf_op jit(solution)/shard_map/ppermute | solution.py:17
  7.0 11.7 %collective-permute-start.2 = (f32[8,128]{1,0:T(8,128)S(1)}, f32[8,128]{1,0:T(8,128)S(1)}, u32[]{:S(2)}, u32[]{:S(2)}) collective-permute-start(f32[8,128]{1,0:T(8,128)S(1)} %fusion.89), channel_id=1, source_target_pairs={{14,0},{0,2},{2,4},{4,6},{6,8},{8,10},{10,12},{12,14},{15,1},{1,3}... | collective-permute-start | bytes 12296 | tf_op jit(solution)/shard_map/ppermute | solution.py:17
  8.5 12.5 %collective-permute-start.3 = (f32[8,128]{1,0:T(8,128)S(1)}, f32[8,128]{1,0:T(8,128)S(1)}, u32[]{:S(2)}, u32[]{:S(2)}) collective-permute-start(f32[8,128]{1,0:T(8,128)S(1)} %fusion.89), channel_id=1, source_target_pairs={{2,0},{4,2},{6,4},{8,6},{10,8},{12,10},{14,12},{0,14},{3,1},{5,3},... | collective-permute-start | bytes 12296 | tf_op jit(solution)/shard_map/ppermute | solution.py:17
  11.7 9.3 %collective-permute-start.4 = (f32[8,128]{1,0:T(8,128)S(1)}, f32[8,128]{1,0:T(8,128)S(1)}, u32[]{:S(2)}, u32[]{:S(2)}) collective-permute-start(f32[8,128]{1,0:T(8,128)S(1)} %fusion.89), channel_id=1, source_target_pairs={{4,0},{6,2},{8,4},{10,6},{12,8},{14,10},{0,12},{2,14},{5,1},{7,3},... | collective-permute-start | bytes 12296 | tf_op jit(solution)/shard_map/ppermute | solution.py:17
  15.7 10.0 %collective-permute-start.5 = (f32[8,128]{1,0:T(8,128)S(1)}, f32[8,128]{1,0:T(8,128)S(1)}, u32[]{:S(2)}, u32[]{:S(2)}) collective-permute-start(f32[8,128]{1,0:T(8,128)S(1)} %fusion.89), channel_id=1, source_target_pairs={{6,0},{8,2},{10,4},{12,6},{14,8},{0,10},{2,12},{4,14},{7,1},{9,3},... | collective-permute-start | bytes 12296 | tf_op jit(solution)/shard_map/ppermute | solution.py:17
  15.8 15.3 %collective-permute-start.6 = (bf16[8,64,128]{2,1,0:T(8,128)(2,1)}, bf16[8,64,128]{2,1,0:T(8,128)(2,1)S(1)}, u32[]{:S(2)}, u32[]{:S(2)}) collective-permute-start(bf16[8,64,128]{2,1,0:T(8,128)(2,1)} %param.15), channel_id=1, source_target_pairs={{10,0},{12,2},{14,4},{0,6},{2,8},{4,10},{6,12},{8,14},{11,1},{13,3... | collective-permute-start | bytes 393224 | tf_op jit(solution)/shard_map/ppermute | solution.py:17
  18.7 12.5 %collective-permute-start.7 = (bf16[8,64,128]{2,1,0:T(8,128)(2,1)}, bf16[8,64,128]{2,1,0:T(8,128)(2,1)S(1)}, u32[]{:S(2)}, u32[]{:S(2)}) collective-permute-start(bf16[8,64,128]{2,1,0:T(8,128)(2,1)} %param.15), channel_id=1, source_target_pairs={{12,0},{14,2},{0,4},{2,6},{4,8},{6,10},{8,12},{10,14},{13,1},{15,3... | collective-permute-start | bytes 393224 | tf_op jit(solution)/shard_map/ppermute | solution.py:17
  21.0 10.2 %collective-permute-start.8 = (bf16[8,64,128]{2,1,0:T(8,128)(2,1)}, bf16[8,64,128]{2,1,0:T(8,128)(2,1)S(1)}, u32[]{:S(2)}, u32[]{:S(2)}) collective-permute-start(bf16[8,64,128]{2,1,0:T(8,128)(2,1)} %param.15), channel_id=1, source_target_pairs={{14,0},{0,2},{2,4},{4,6},{6,8},{8,10},{10,12},{12,14},{15,1},{1,3}... | collective-permute-start | bytes 393224 | tf_op jit(solution)/shard_map/ppermute | solution.py:17
  21.0 10.3 %collective-permute-start.9 = (bf16[8,64,128]{2,1,0:T(8,128)(2,1)}, bf16[8,64,128]{2,1,0:T(8,128)(2,1)S(1)}, u32[]{:S(2)}, u32[]{:S(2)}) collective-permute-start(bf16[8,64,128]{2,1,0:T(8,128)(2,1)} %param.15), channel_id=1, source_target_pairs={{2,0},{4,2},{6,4},{8,6},{10,8},{12,10},{14,12},{0,14},{3,1},{5,3},... | collective-permute-start | bytes 393224 | tf_op jit(solution)/shard_map/ppermute | solution.py:17
  31.1 6.1 %collective-permute-start.11 = (bf16[8,64,128]{2,1,0:T(8,128)(2,1)}, bf16[8,64,128]{2,1,0:T(8,128)(2,1)S(1)}, u32[]{:S(2)}, u32[]{:S(2)}) collective-permute-start(bf16[8,64,128]{2,1,0:T(8,128)(2,1)} %param.15), channel_id=1, source_target_pairs={{6,0},{8,2},{10,4},{12,6},{14,8},{0,10},{2,12},{4,14},{7,1},{9,3},... | collective-permute-start | bytes 393224 | tf_op jit(solution)/shard_map/ppermute | solution.py:17
  161.4 6.0 %collective-permute-start.12 = (f32[8,128]{1,0:T(8,128)S(1)}, f32[8,128]{1,0:T(8,128)S(1)}, u32[]{:S(2)}, u32[]{:S(2)}) collective-permute-start(f32[8,128]{1,0:T(8,128)S(1)} %get-tuple-element.306), channel_id=1, source_target_pairs={{6,0},{8,2},{10,4},{12,6},{14,8},{0,10},{2,12},{4,14},{7,1},{9,3},... | collective-permute-start | bytes 12296 | tf_op jit(solution)/shard_map/ppermute | solution.py:17
  162.4 7.1 %collective-permute-start.13 = (f32[8,128]{1,0:T(8,128)S(1)}, f32[8,128]{1,0:T(8,128)S(1)}, u32[]{:S(2)}, u32[]{:S(2)}) collective-permute-start(f32[8,128]{1,0:T(8,128)S(1)} %get-tuple-element.311), channel_id=1, source_target_pairs={{4,0},{6,2},{8,4},{10,6},{12,8},{14,10},{0,12},{2,14},{5,1},{7,3},... | collective-permute-start | bytes 12296 | tf_op jit(solution)/shard_map/ppermute | solution.py:17
  163.7 5.8 %collective-permute-start.14 = (f32[8,128]{1,0:T(8,128)S(1)}, f32[8,128]{1,0:T(8,128)S(1)}, u32[]{:S(2)}, u32[]{:S(2)}) collective-permute-start(f32[8,128]{1,0:T(8,128)S(1)} %get-tuple-element.310), channel_id=1, source_target_pairs={{2,0},{4,2},{6,4},{8,6},{10,8},{12,10},{14,12},{0,14},{3,1},{5,3},... | collective-permute-start | bytes 12296 | tf_op jit(solution)/shard_map/ppermute | solution.py:17
  166.8 6.3 %collective-permute-start.15 = (f32[8,128]{1,0:T(8,128)S(1)}, f32[8,128]{1,0:T(8,128)S(1)}, u32[]{:S(2)}, u32[]{:S(2)}) collective-permute-start(f32[8,128]{1,0:T(8,128)S(1)} %get-tuple-element.309), channel_id=1, source_target_pairs={{14,0},{0,2},{2,4},{4,6},{6,8},{8,10},{10,12},{12,14},{15,1},{1,3}... | collective-permute-start | bytes 12296 | tf_op jit(solution)/shard_map/ppermute | solution.py:17
  166.8 6.3 %collective-permute-start.16 = (f32[8,128]{1,0:T(8,128)S(1)}, f32[8,128]{1,0:T(8,128)S(1)}, u32[]{:S(2)}, u32[]{:S(2)}) collective-permute-start(f32[8,128]{1,0:T(8,128)S(1)} %get-tuple-element.308), channel_id=1, source_target_pairs={{12,0},{14,2},{0,4},{2,6},{4,8},{6,10},{8,12},{10,14},{13,1},{15,3... | collective-permute-start | bytes 12296 | tf_op jit(solution)/shard_map/ppermute | solution.py:17
  167.4 6.3 %collective-permute-start.17 = (f32[8,128]{1,0:T(8,128)S(1)}, f32[8,128]{1,0:T(8,128)S(1)}, u32[]{:S(2)}, u32[]{:S(2)}) collective-permute-start(f32[8,128]{1,0:T(8,128)S(1)} %get-tuple-element.307), channel_id=1, source_target_pairs={{10,0},{12,2},{14,4},{0,6},{2,8},{4,10},{6,12},{8,14},{11,1},{13,3... | collective-permute-start | bytes 12296 | tf_op jit(solution)/shard_map/ppermute | solution.py:17
  175.8 8.9 %collective-permute-start.18 = (f32[8,128]{1,0:T(8,128)S(1)}, f32[8,128]{1,0:T(8,128)S(1)}, u32[]{:S(2)}, u32[]{:S(2)}) collective-permute-start(f32[8,128]{1,0:T(8,128)S(1)} %select_select_fusion), channel_id=1, source_target_pairs={{10,0},{12,2},{14,4},{0,6},{2,8},{4,10},{6,12},{8,14},{11,1},{13,3... | collective-permute-start | bytes 12296 | tf_op jit(solution)/shard_map/ppermute | solution.py:17
  176.2 9.1 %collective-permute-start.19 = (f32[8,128]{1,0:T(8,128)S(1)}, f32[8,128]{1,0:T(8,128)S(1)}, u32[]{:S(2)}, u32[]{:S(2)}) collective-permute-start(f32[8,128]{1,0:T(8,128)S(1)} %select_select_fusion), channel_id=1, source_target_pairs={{12,0},{14,2},{0,4},{2,6},{4,8},{6,10},{8,12},{10,14},{13,1},{15,3... | collective-permute-start | bytes 12296 | tf_op jit(solution)/shard_map/ppermute | solution.py:17
  179.3 6.3 %collective-permute-start.20 = (f32[8,128]{1,0:T(8,128)S(1)}, f32[8,128]{1,0:T(8,128)S(1)}, u32[]{:S(2)}, u32[]{:S(2)}) collective-permute-start(f32[8,128]{1,0:T(8,128)S(1)} %select_select_fusion), channel_id=1, source_target_pairs={{14,0},{0,2},{2,4},{4,6},{6,8},{8,10},{10,12},{12,14},{15,1},{1,3}... | collective-permute-start | bytes 12296 | tf_op jit(solution)/shard_map/ppermute | solution.py:17
  311.1 7.4 %collective-permute-start.24 = (f32[8,128]{1,0:T(8,128)S(1)}, f32[8,128]{1,0:T(8,128)S(1)}, u32[]{:S(2)}, u32[]{:S(2)}) collective-permute-start(f32[8,128]{1,0:T(8,128)S(1)} %get-tuple-element.300), channel_id=1, source_target_pairs={{6,0},{8,2},{10,4},{12,6},{14,8},{0,10},{2,12},{4,14},{7,1},{9,3},... | collective-permute-start | bytes 12296 | tf_op jit(solution)/shard_map/ppermute | solution.py:17
  312.6 8.2 %collective-permute-start.25 = (f32[8,128]{1,0:T(8,128)S(1)}, f32[8,128]{1,0:T(8,128)S(1)}, u32[]{:S(2)}, u32[]{:S(2)}) collective-permute-start(f32[8,128]{1,0:T(8,128)S(1)} %get-tuple-element.305), channel_id=1, source_target_pairs={{4,0},{6,2},{8,4},{10,6},{12,8},{14,10},{0,12},{2,14},{5,1},{7,3},... | collective-permute-start | bytes 12296 | tf_op jit(solution)/shard_map/ppermute | solution.py:17
  315.0 5.8 %collective-permute-start.26 = (f32[8,128]{1,0:T(8,128)S(1)}, f32[8,128]{1,0:T(8,128)S(1)}, u32[]{:S(2)}, u32[]{:S(2)}) collective-permute-start(f32[8,128]{1,0:T(8,128)S(1)} %get-tuple-element.304), channel_id=1, source_target_pairs={{2,0},{4,2},{6,4},{8,6},{10,8},{12,10},{14,12},{0,14},{3,1},{5,3},... | collective-permute-start | bytes 12296 | tf_op jit(solution)/shard_map/ppermute | solution.py:17
  316.3 6.3 %collective-permute-start.27 = (f32[8,128]{1,0:T(8,128)S(1)}, f32[8,128]{1,0:T(8,128)S(1)}, u32[]{:S(2)}, u32[]{:S(2)}) collective-permute-start(f32[8,128]{1,0:T(8,128)S(1)} %get-tuple-element.303), channel_id=1, source_target_pairs={{14,0},{0,2},{2,4},{4,6},{6,8},{8,10},{10,12},{12,14},{15,1},{1,3}... | collective-permute-start | bytes 12296 | tf_op jit(solution)/shard_map/ppermute | solution.py:17
  (10 other events, 166.3 us)
where the time goes:
time: 331 us; the launch traced here: 326 us
  matrix products  156 us (47%)
  other arithmetic  92.6 us (28%)
  starting transfers between devices  47.8 us (14%)
  waiting for transfers between devices  17 us (5%)
  local copies, waits for them, and re-layouts  5.98 us (2%)
  blocking collectives  3.78 us (1%)
    dot_general x64, matrix products, block_cost(): jnp.einsum('dr,kdc->krc', source, targets, preferred_element_type=jnp.flo...  153 us
    ppermute x30, starting transfers between devices, passed_along(): return lax.ppermute(block, axis, route)  47.8 us
    reduce_sum x2, other arithmetic, local(): jnp.sum(jnp.where(flat_pick[:, :, None], window_peak[None, :, :], 0.0), a...  29.6 us
    reduce_sum x32, other arithmetic, row_block(): jnp.sum(jnp.where(allowed, jnp.exp(scores - row_peak[None, :, None]), 0.0...  19.8 us
    ppermute x30, waiting for transfers between devices, passed_along(): return lax.ppermute(block, axis, route)  17 us
    reduce_sum x32, other arithmetic, column_block(): jnp.sum(jnp.where(allowed, jnp.exp(scores - col_peak[:, None, :]), 0.0),...  9.9 us
    reduce_sum x2, other arithmetic, local(): jnp.sum(jnp.where(slot_pick[:, :, :, None], window_potential[None, None,...  9.8 us
    reduce_max x2, other arithmetic, local(): jnp.max(jnp.where(flat_pick.T[:, :, None], partial_value[None, :, :], FIL...  9.15 us
  transfers between devices with their start and end apart: 30, of which 8 were waited for; matrix products, arithmetic and copies ran while one was open for 3% of the time, Pallas kernels for 0%

commit v1 on v0

v1 whole, which is shorter than its diff:
```python
import functools
import math

import jax
import jax.numpy as jnp
from jax import lax
from jax.experimental import pallas as pl
from jax.experimental.pallas import tpu as pltpu
from jax.sharding import PartitionSpec as P

REACH = 3
ITERS = 2
EPSILON = 0.05
SCALE = math.log2(math.e) / EPSILON
DEAD = -1e30
EMPTY = -1e38
UNROLL = 4
STEP = 32


def half_step_kernel(
    final, idx_ref, len_ref, cnt_ref, src_ref, pts_ref, pot_ref, *refs
):
    if final:
        fld_ref, out_ref, add_ref, sco_ref, peak_ref, sum_ref = refs
    else:
        fld_ref = None
        out_ref, add_ref, sco_ref, peak_ref, sum_ref = refs
    blocks, feat, cells = src_ref.shape
    targets = pot_ref.shape[0]
    f32, bf16 = jnp.float32, jnp.bfloat16

    rows16 = lax.broadcasted_iota(jnp.int32, (16, cells), 0)

    def spread(t, carry):
        pot = pot_ref[pl.ds(t, 1), :]
        hi = pot.astype(bf16).astype(f32)
        rest = pot - hi
        mid = rest.astype(bf16).astype(f32)
        low = rest - mid
        tile = jnp.where(rows16 == 0, hi, jnp.where(rows16 == 1, mid, jnp.where(rows16 == 2, low, 0.0)))
        add_ref[t] = tile.astype(bf16)
        return carry

    lax.fori_loop(0, targets, spread, 0, unroll=8)
    add_ref[targets] = jnp.where(rows16 == 0, DEAD, 0.0).astype(bf16)
    peak_ref[...] = jnp.full(peak_ref.shape, EMPTY, f32)
    sum_ref[...] = jnp.zeros(sum_ref.shape, f32)

    def source_block(i, rows):
        length = len_ref[i]
        count = cnt_ref[i]
        groups = (length + (UNROLL - 1)) // UNROLL
        source = src_ref[i].astype(f32)
        scaled = source * (2.0 * SCALE)
        hi = scaled.astype(bf16).astype(f32)
        low = scaled - hi
        both = jnp.concatenate([hi, low], axis=0).T.astype(bf16)[:rows]
        ones = (lax.broadcasted_iota(jnp.int32, (rows, 16), 1) < 3).astype(f32).astype(bf16)
        left = jnp.concatenate([both, ones], axis=1)

        def pick(k):
            live = k < length
            t = idx_ref[i, jnp.minimum(k, length - 1)]
            return t, jnp.where(live, t, targets)

        def score_group(g, peak):
            for u in range(UNROLL):
                k = g * UNROLL + u
                t, ta = pick(k)
                right = jnp.concatenate([pts_ref[t], pts_ref[t], add_ref[ta]], axis=0)
                score = jnp.dot(left, right, preferred_element_type=f32)
                sco_ref[k, :rows, :] = score
                peak = jnp.maximum(peak, score)
            return peak

        peak = lax.fori_loop(0, groups, score_group, jnp.full((rows, cells), EMPTY, f32))
        top = jnp.max(peak, axis=1, keepdims=True)

        def row_group(g, total):
            for u in range(UNROLL):
                total += jnp.exp2(sco_ref[g * UNROLL + u, :rows, :] - top)
            return total

        total = lax.fori_loop(0, groups, row_group, jnp.zeros((rows, cells), f32))
        row_lse = top + jnp.log2(jnp.sum(total, axis=1, keepdims=True))
        row_iota = lax.broadcasted_iota(jnp.int32, (rows, 1), 0)
        shift = jnp.where(row_iota < count, -row_lse, DEAD)

        if final:
            diag = lax.broadcasted_iota(jnp.int32, (rows, cells), 0) == lax.broadcasted_iota(
                jnp.int32, (rows, cells), 1
            )
            flat = jnp.sum(jnp.where(diag, row_lse, 0.0), axis=0, keepdims=True)
            squares = jnp.sum(source * source, axis=0, keepdims=True)
            lane = lax.broadcasted_iota(jnp.int32, (1, cells), 1)
            fld_ref[pl.ds(i, 1), :] = jnp.where(lane < count, squares - flat * (1.0 / SCALE), 0.0)

        def column_group(g, carry):
            for u in range(UNROLL):
                k = g * UNROLL + u
                _, ta = pick(k)
                shifted = (sco_ref[k, :rows, :] + shift).reshape(rows // 8, 8, cells)
                top8 = jnp.max(shifted, axis=0)
                sum8 = jnp.sum(jnp.exp2(shifted - top8[None]), axis=0)
                old = peak_ref[ta]
                new = jnp.maximum(old, top8)
                peak_ref[ta] = new
                sum_ref[ta] = sum_ref[ta] * jnp.exp2(old - new) + sum8 * jnp.exp2(top8 - new)
            return carry

        lax.fori_loop(0, groups, column_group, 0)

    def each_block(i, carry):
        steps = (cnt_ref[i] + (STEP - 1)) // STEP
        for s in range(1, cells // STEP + 1):

            @pl.when(steps == s)
            def _():
                source_block(i, s * STEP)

        return carry

    lax.fori_loop(0, blocks, each_block, 0)

    peak = peak_ref[:targets]
    top = jnp.max(peak, axis=1, keepdims=True)
    total = jnp.sum(sum_ref[:targets] * jnp.exp2(peak - top), axis=1)
    out_ref[...] = jnp.maximum(top[:, 0, :] + jnp.log2(total), EMPTY)


def half_step(final, block_list, list_len, src_counts, src_points, pts, pot):
    blocks, feat, cells = src_points.shape
    targets = pot.shape[0]
    slots = -(-block_list.shape[1] // UNROLL) * UNROLL
    smem = pl.BlockSpec(memory_space=pltpu.SMEM)
    vmem = pl.BlockSpec(memory_space=pltpu.VMEM)
    outs = [jax.ShapeDtypeStruct((targets, cells), jnp.float32)]
    if final:
        outs = [jax.ShapeDtypeStruct((blocks, cells), jnp.float32)] + outs
    return pl.pallas_call(
        functools.partial(half_step_kernel, final),
        out_shape=outs,
        in_specs=[smem, smem, smem, vmem, vmem, vmem],
        out_specs=[vmem] * len(outs),
        scratch_shapes=[
            pltpu.VMEM((targets + 1, 16, cells), jnp.bfloat16),
            pltpu.VMEM((slots, cells, cells), jnp.float32),
            pltpu.VMEM((targets + 1, 8, cells), jnp.float32),
            pltpu.VMEM((targets + 1, 8, cells), jnp.float32),
        ],
        compiler_params=pltpu.CompilerParams(vmem_limit_bytes=40 * 1024 * 1024),
    )(block_list, list_len, src_counts, src_points, pts, pot)


def local(src_points, tgt_points, block_list, list_len, src_counts, tgt_counts):
    loop_index = lax.axis_index("loop")
    tgt_blocks, _, cells = tgt_points.shape
    tgt_valid = jnp.arange(cells)[None, :] < tgt_counts[:, None]
    squares = jnp.sum(jnp.square(tgt_points.astype(jnp.float32)), axis=1)
    pot_home = jnp.where(tgt_valid, -SCALE * squares, DEAD)
    pts = lax.all_gather(tgt_points, "loop", tiled=True)
    pot = lax.all_gather(pot_home, "loop", tiled=True)
    for it in range(ITERS):
        final = it == ITERS - 1
        res = half_step(final, block_list, list_len, src_counts, src_points, pts, pot)
        every = lax.all_gather(res[-1], ("loop", "narrow"))
        top = jnp.max(every, axis=0)
        lse = top + jnp.log2(jnp.sum(jnp.exp2(every - top[None]), axis=0))
        pot = jnp.where(pot > 0.1 * DEAD, pot - lse, DEAD)
    mine = lax.dynamic_slice_in_dim(pot, loop_index * tgt_blocks, tgt_blocks, 0)
    tgt_field = jnp.where(tgt_valid, mine * (1.0 / SCALE) + squares, 0.0)
    return res[0], tgt_field


def solution(mesh):
    placed = (
        P(("groups", "loop", "narrow"), None, None),
        P(("groups", "loop"), None, None),
        P(("groups", "loop", "narrow"), None),
        P(("groups", "loop", "narrow")),
        P(("groups", "loop", "narrow")),
        P(("groups", "loop")),
    )
    return jax.shard_map(
        local,
        mesh=mesh,
        in_specs=placed,
        out_specs=(P(("groups", "loop", "narrow"), None), P(("groups", "loop"), None)),
        check_vma=False,
    )
```

time: 331 us -> 147 us (0.44); the launches traced: 326 us -> 147 us
  matrix products: 156 us -> 0 us
  other arithmetic: 92.6 us -> 1.97 us
  blocking collectives: 3.78 us -> 81.3 us
  starting transfers between devices: 47.8 us -> 0.04 us
  Pallas kernels: 0 us -> 35.9 us
  between operations: 1.04 us -> 14.1 us
  local copies, waits for them, and re-layouts: 5.98 us -> 1.24 us
  waiting for transfers between devices: 17 us -> 12.3 us
    dot_general x67 -> x0, matrix products: 156 us -> none  [the longest x64 153 us: block_cost(): jnp.einsum('dr,kdc->krc', source, targets, preferred_element_type=jnp.flo...]
    all_gather x2 -> x3, blocking collectives: 3.78 us -> 81.3 us  [the longest x2 48.9 us: local(): every = lax.all_gather(res[-1], ('loop', 'narrow'))]
    reduce_sum x70 -> x3, other arithmetic: 73.1 us -> 1.14 us  [the longest x1 0.95 us: local(): squares = jnp.sum(jnp.square(tgt_points.astype(jnp.float32)), axis=1)]
    ppermute x30 -> x0, starting transfers between devices: 47.8 us -> none  [passed_along(): return lax.ppermute(block, axis, route)]
    pallas_call x0 -> x2, Pallas kernels: none -> 35.9 us  [half_step(): pl.pallas_call(functools.partial(half_step_kernel, final), out_shape=outs...]
    ppermute x30 -> x0, waiting for transfers between devices: 17 us -> none  [passed_along(): return lax.ppermute(block, axis, route)]
    all_gather x0 -> x1, waiting for transfers between devices: none -> 11.6 us  [local(): pts = lax.all_gather(tgt_points, 'loop', tiled=True)]
    reduce_max x2, other arithmetic: 9.15 us -> 0.07 us  [local(): top = jnp.max(every, axis=0)]
  transfers between devices with their start and end apart: 30 -> 1, of which waited for: 8 -> 1; matrix products, arithmetic and copies ran while one was open for 3% -> 1% of each run, Pallas kernels for 0% -> 0%
where the time goes in v1:
time: 147 us
  blocking collectives  81.3 us (55%)
  Pallas kernels  35.9 us (24%)
  between operations  14.1 us (10%)
  waiting for transfers between devices  12.3 us (8%)
  other arithmetic  1.97 us (1%)
    all_gather x2, blocking collectives, local(): every = lax.all_gather(res[-1], ('loop', 'narrow'))  48.9 us
    pallas_call x2, Pallas kernels, half_step(): pl.pallas_call(functools.partial(half_step_kernel, final), out_shape=outs...  35.9 us
    all_gather x1, blocking collectives, local(): pot = lax.all_gather(pot_home, 'loop', tiled=True)  32.4 us
    all_gather x1, waiting for transfers between devices, local(): pts = lax.all_gather(tgt_points, 'loop', tiled=True)  11.6 us
  transfers between devices with their start and end apart: 1, of which 1 were waited for; matrix products, arithmetic and copies ran while one was open for 1% of the time, Pallas kernels for 0%

profile of v1, /device:TPU:0, one launch (start us, length us, event | category | flops | bytes accessed | tf_op | source)
XLA Modules:
  0.0 146.8 jit_solution(2950295250983750185)
XLA Ops:
  7.2 0.0 copy-start.2
  7.2 0.0 all-gather.4.cloned.1.call-start
  7.2 0.7 all-gather.4.cloned.1.call-update
  7.9 0.0 copy-start.6
  7.9 0.9 multiply_reduce_fusion
  8.9 0.0 copy-done.6
  8.9 0.1 multiply_select_fusion
  9.0 32.4 %all_gather.19.pot_ref = f32[64,128]{1,0:T(8,128)S(1)} all-gather(f32[8,128]{1,0:T(8,128)S(1)} %multiply_select_fusion), channel_id=1, replica_groups=mesh['groups'=2,'loop'=8,'narrow'=2] {'loop'}, dimensions={0}, use_global_device_ids=true | all-gather | bytes 36864 | tf_op jit(solution)/shard_map/all_gather | solution.py:163
  41.4 11.6 %all-gather.4.cloned.1.call-done.pts_ref = bf16[64,64,128]{2,1,0:T(8,128)(2,1)} async-done(((bf16[8,64,128]{2,1,0:T(8,128)(2,1)}), bf16[64,64,128]{2,1,0:T(8,128)(2,1)}) %all-gather.4.cloned.1.call-update) | async-done | bytes 1048592 | tf_op jit(solution)/shard_map/all_gather | solution.py:162
  52.9 0.0 copy-done.2
  52.9 0.0 copy-done.3
  53.0 0.0 copy-done.4
  53.0 0.0 copy-done.5
  53.0 0.0 copy-start
  53.0 1.2 copy-done
  54.2 17.7 %shard_map.77 = f32[64,128]{1,0:T(8,128)S(1)} custom-call(s32[16,24]{1,0:T(8,128)S(1)} %copy-done.3, s32[16]{0:T(128)S(1)} %copy-done.4, s32[16]{0:T(128)S(1)} %copy-done.5, bf16[16,64,128]{2,1,0:T(8,128)(2,1)S(1)} %copy-done.2, bf16[64,64,128]{2,1,0:T(8,128)(2,1)S(1)} %copy-done, f32[64,128]{1,0:T(8,128)S(1)} %all_gather.19.pot_ref), custom_call_target="tpu_custom_call" | custom-call | tf_op jit(solution)/shard_map/pallas_call | solution.py:141
  71.9 0.0 copy-start.1
  71.9 24.8 %all-gather = f32[1024,128]{1,0:T(8,128)S(1)} all-gather(f32[64,128]{1,0:T(8,128)S(1)} %shard_map.77), channel_id=2, replica_groups=mesh['groups'=2,'loop'=8,'narrow'=2] {'loop','narrow'}, dimensions={0}, use_global_device_ids=true | all-gather | bytes 557056 | tf_op jit(solution)/shard_map/all_gather | solution.py:167
  96.7 0.1 exponential_reduce_fusion.1
  96.9 0.0 copy-done.1
  96.9 18.2 %shard_map.78 = (f32[16,128]{1,0:T(8,128)}, f32[64,128]{1,0:T(8,128)S(1)}) custom-call(s32[16,24]{1,0:T(8,128)S(1)} %copy-done.3, s32[16]{0:T(128)S(1)} %copy-done.4, s32[16]{0:T(128)S(1)} %copy-done.5, bf16[16,64,128]{2,1,0:T(8,128)(2,1)S(1)} %copy-done.2, bf16[64,64,128]{2,1,0:T(8,128)(2,1)S(1)} %copy-done.1, f32[64,128]{1,0:T(8,128)S(1)} %subtract_select_fusion.pot_ref), custom_call_target="tpu_custom_call" | custom-call | tf_op jit(solution)/shard_map/pallas_call | solution.py:141
  115.1 24.0 %all-gather.1 = f32[1024,128]{1,0:T(8,128)S(1)} all-gather(f32[64,128]{1,0:T(8,128)S(1)} %get-tuple-element.5), channel_id=3, replica_groups=mesh['groups'=2,'loop'=8,'narrow'=2] {'loop','narrow'}, dimensions={0}, use_global_device_ids=true | all-gather | bytes 557056 | tf_op jit(solution)/shard_map/all_gather | solution.py:167
  139.2 0.1 exponential_reduce_fusion
  139.3 0.7 fusion.4
  (6 shorter events, 0.1 us)
Async XLA Ops:
  7.2 45.8 %copy-start.2 = (bf16[16,64,128]{2,1,0:T(8,128)(2,1)S(1)}, bf16[16,64,128]{2,1,0:T(8,128)(2,1)}, u32[]{:S(2)}) copy-start(bf16[16,64,128]{2,1,0:T(8,128)(2,1)} %src_ref.3) | copy-start | bytes 786436
  7.2 45.8 %all-gather.4.cloned.1.call-start = ((), (), s32[]{:S(2)}) async-start(), calls=%async_computation | async-start | bytes 1179648 | tf_op jit(solution)/shard_map/all_gather | solution.py:162
  7.9 1.0 copy-start.6
  9.0 44.0 %copy-start.3 = (s32[16,24]{1,0:T(8,128)S(1)}, s32[16,24]{1,0:T(8,128)}, u32[]{:S(2)}) copy-start(s32[16,24]{1,0:T(8,128)} %idx_ref.3) | copy-start | bytes 4612
  9.0 44.0 %copy-start.4 = (s32[16]{0:T(128)S(1)}, s32[16]{0:T(128)}, u32[]{:S(2)}) copy-start(s32[16]{0:T(128)} %len_ref.3) | copy-start | bytes 196
  9.0 44.0 %copy-start.5 = (s32[16]{0:T(128)S(1)}, s32[16]{0:T(128)}, u32[]{:S(2)}) copy-start(s32[16]{0:T(128)} %cnt_ref.3) | copy-start | bytes 196
  53.0 1.2 copy-start
  71.9 25.0 %copy-start.1 = (bf16[64,64,128]{2,1,0:T(8,128)(2,1)S(1)}, bf16[64,64,128]{2,1,0:T(8,128)(2,1)}, u32[]{:S(2)}) copy-start(bf16[64,64,128]{2,1,0:T(8,128)(2,1)} %all-gather.4.cloned.1.call-done.pts_ref) | copy-start | bytes 3145732
Sparse Core Ops, SparseCore 0:
  10.1 42.7 all-gather.3

commit v2 on v1

--- a/solution.py
+++ b/solution.py
@@ -153,24 +153,186 @@
     )(block_list, list_len, src_counts, src_points, pts, pot)
 
 
+MESH = pl.DeviceIdType.MESH
+OFFSETS = tuple(d for d in range(-REACH, REACH + 1) if d != 0)
+
+
+def place(distance):
+    loop = lax.axis_size("loop")
+    return lax.rem(lax.axis_index("loop") + (distance + loop), loop)
+
+
+def greet(peers):
+    barrier = pltpu.get_barrier_semaphore()
+    for peer in peers:
+        pl.semaphore_signal(barrier, inc=1, device_id=peer, device_id_type=MESH)
+    pl.semaphore_wait(barrier, len(peers))
+
+
+def remote(src, dst, send_sem, recv_sem, peer):
+    return pltpu.make_async_remote_copy(
+        src_ref=src, dst_ref=dst, send_sem=send_sem, recv_sem=recv_sem,
+        device_id=peer, device_id_type=MESH,
+    )
+
+
+def gather_kernel(
+    cnt_ref, tgt_ref, pts_ref, pot_ref,
+    send_sem, recv_sem, pot_send, pot_recv, pass_send, pass_recv, own_sem,
+):
+    me, core = lax.axis_index("loop"), lax.axis_index("narrow")
+    other = 1 - core
+    blocks, feat, cells = tgt_ref.shape
+    half = blocks // 2
+    greet([{"loop": place(d), "narrow": core} for d in OFFSETS] + [{"loop": me, "narrow": other}])
+
+    def part(home, which):
+        return pts_ref.at[pl.ds(home * blocks + which * half, half)]
+
+    sends = []
+    for j, d in enumerate(OFFSETS):
+        copy = remote(
+            tgt_ref.at[pl.ds(core * half, half)], part(me, core),
+            send_sem.at[j], recv_sem.at[j], {"loop": place(d), "narrow": core},
+        )
+        copy.start()
+        sends.append(copy)
+    own = pltpu.make_async_copy(tgt_ref, pts_ref.at[pl.ds(me * blocks, blocks)], own_sem)
+    own.start()
+
+    lane = lax.broadcasted_iota(jnp.int32, (1, cells), 1)
+    rows = []
+    for b in range(blocks):
+        cell = tgt_ref[b].astype(jnp.float32)
+        square = jnp.sum(cell * cell, axis=0, keepdims=True)
+        rows.append(jnp.where(lane < cnt_ref[b], -SCALE * square, DEAD))
+    mine = pot_ref.at[pl.ds(pl.multiple_of(me * blocks, 8), blocks)]
+    mine[...] = jnp.concatenate(rows, axis=0)
+    for j, d in enumerate(OFFSETS):
+        copy = remote(mine, mine, pot_send.at[j], pot_recv.at[j], {"loop": place(d), "narrow": core})
+        copy.start()
+        sends.append(copy)
+
+    partner = {"loop": me, "narrow": other}
+    passed = []
+    for j, d in enumerate(OFFSETS):
+        got = part(place(-d), core)
+        remote(got, got, send_sem.at[j], recv_sem.at[j], partner).wait_recv()
+        copy = remote(got, got, pass_send.at[j], pass_recv.at[j], partner)
+        copy.start()
+        passed.append(copy)
+    for j, d in enumerate(OFFSETS):
+        home = place(-d)
+        got = part(home, other)
+        remote(got, got, pass_send.at[j], pass_recv.at[j], partner).wait_recv()
+        got = pot_ref.at[pl.ds(pl.multiple_of(home * blocks, 8), blocks)]
+        remote(got, got, pot_send.at[j], pot_recv.at[j], partner).wait_recv()
+    for copy in sends + passed:
+        copy.wait_send()
+    own.wait()
+
+
+def gather(tgt_counts, tgt_points):
+    blocks, feat, cells = tgt_points.shape
+    targets = blocks * lax.axis_size("loop")
+    vmem = pl.BlockSpec(memory_space=pltpu.VMEM)
+    dma = pltpu.SemaphoreType.DMA
+    n = len(OFFSETS)
+    return pl.pallas_call(
+        gather_kernel,
+        out_shape=[
+            jax.ShapeDtypeStruct((targets, feat, cells), tgt_points.dtype),
+            jax.ShapeDtypeStruct((targets, cells), jnp.float32),
+        ],
+        in_specs=[pl.BlockSpec(memory_space=pltpu.SMEM), vmem],
+        out_specs=[vmem, vmem],
+        scratch_shapes=[dma((n,))] * 6 + [dma],
+        compiler_params=pltpu.CompilerParams(
+            collective_id=0, has_side_effects=True, vmem_limit_bytes=24 * 1024 * 1024
+        ),
+    )(tgt_counts, tgt_points)
+
+
+def exchange_kernel(
+    last, cnt_ref, lse_ref, pot_ref, *refs
+):
+    if last:
+        base_ref, out_ref, inbox, send_sem, recv_sem = refs
+    else:
+        out_ref, inbox, send_sem, recv_sem, pot_send, pot_recv = refs
+    me, core = lax.axis_index("loop"), lax.axis_index("narrow")
+    blocks = cnt_ref.shape[0]
+    cells = lse_ref.shape[1]
+    routes = [(d, side) for d in (0,) + OFFSETS for side in (0, 1) if (d, side) != (0, 0)]
+    peers = [{"loop": place(d), "narrow": lax.rem(core + side, 2)} for d, side in routes]
+    greet(peers)
+
+    def rows(ref, home):
+        return ref.at[pl.ds(pl.multiple_of(home * blocks, 8), blocks)]
+
+    sends = []
+    for j, (d, side) in enumerate(routes):
+        copy = remote(rows(lse_ref, place(d)), inbox.at[j], send_sem.at[j], recv_sem.at[j], peers[j])
+        copy.start()
+        sends.append(copy)
+    lane = lax.broadcasted_iota(jnp.int32, (1, cells), 1)
+    lane = jnp.broadcast_to(lane, (blocks, cells))
+    sub = lax.broadcasted_iota(jnp.int32, (blocks, cells), 0)
+    live = lane < cnt_ref[0]
+    for b in range(1, blocks):
+        live = jnp.where(sub == b, (lane < cnt_ref[b]).astype(jnp.int32), live.astype(jnp.int32)) > 0
+    for j in range(len(routes)):
+        sends[j].wait_recv()
+    top = own = rows(lse_ref, me)[...]
+    for j in range(len(routes)):
+        top = jnp.maximum(top, inbox[j])
+    total = jnp.exp2(own - top)
+    for j in range(len(routes)):
+        total += jnp.exp2(inbox[j] - top)
+    pot = rows(pot_ref, me)[...] - (top + jnp.log2(total))
+    if last:
+        out_ref[...] = jnp.where(live, (pot - rows(base_ref, me)[...]) * (1.0 / SCALE), 0.0)
+    else:
+        mine = rows(out_ref, me)
+        mine[...] = jnp.where(live, pot, DEAD)
+        for j, d in enumerate(OFFSETS):
+            copy = remote(mine, mine, pot_send.at[j], pot_recv.at[j], {"loop": place(d), "narrow": core})
+            copy.start()
+            sends.append(copy)
+        for j, d in enumerate(OFFSETS):
+            got = rows(out_ref, place(-d))
+            remote(got, got, pot_send.at[j], pot_recv.at[j], {"loop": me, "narrow": 1 - core}).wait_recv()
+    for copy in sends:
+        copy.wait_send()
+
+
+def exchange(last, tgt_counts, lse, pot, *base):
+    targets, cells = lse.shape
+    blocks = tgt_counts.shape[0]
+    vmem = pl.BlockSpec(memory_space=pltpu.VMEM)
+    dma = pltpu.SemaphoreType.DMA
+    n = 2 * len(OFFSETS) + 1
+    return pl.pallas_call(
+        functools.partial(exchange_kernel, last),
+        out_shape=jax.ShapeDtypeStruct((blocks if last else targets, cells), jnp.float32),
+        in_specs=[pl.BlockSpec(memory_space=pltpu.SMEM)] + [vmem] * (2 + len(base)),
+        out_specs=vmem,
+        scratch_shapes=[pltpu.VMEM((n, blocks, cells), jnp.float32), dma((n,)), dma((n,))]
+        + ([] if last else [dma((len(OFFSETS),))] * 2),
+        compiler_params=pltpu.CompilerParams(collective_id=2 if last else 1, has_side_effects=True),
+    )(tgt_counts, lse, pot, *base)
+
+
 def local(src_points, tgt_points, block_list, list_len, src_counts, tgt_counts):
-    loop_index = lax.axis_index("loop")
-    tgt_blocks, _, cells = tgt_points.shape
-    tgt_valid = jnp.arange(cells)[None, :] < tgt_counts[:, None]
-    squares = jnp.sum(jnp.square(tgt_points.astype(jnp.float32)), axis=1)
-    pot_home = jnp.where(tgt_valid, -SCALE * squares, DEAD)
-    pts = lax.all_gather(tgt_points, "loop", tiled=True)
-    pot = lax.all_gather(pot_home, "loop", tiled=True)
-    for it in range(ITERS):
-        final = it == ITERS - 1
-        res = half_step(final, block_list, list_len, src_counts, src_points, pts, pot)
-        every = lax.all_gather(res[-1], ("loop", "narrow"))
-        top = jnp.max(every, axis=0)
-        lse = top + jnp.log2(jnp.sum(jnp.exp2(every - top[None]), axis=0))
-        pot = jnp.where(pot > 0.1 * DEAD, pot - lse, DEAD)
-    mine = lax.dynamic_slice_in_dim(pot, loop_index * tgt_blocks, tgt_blocks, 0)
-    tgt_field = jnp.where(tgt_valid, mine * (1.0 / SCALE) + squares, 0.0)
-    return res[0], tgt_field
+    pts, first = gather(tgt_counts, tgt_points)
+    listed = (block_list, list_len, src_counts, src_points, pts)
+    (lse,) = half_step(False, *listed, first)
+    pot = exchange(False, tgt_counts, lse, first)
+    for it in range(1, ITERS - 1):
+        (lse,) = half_step(False, *listed, pot)
+        pot = exchange(False, tgt_counts, lse, pot)
+    src_field, lse = half_step(True, *listed, pot)
+    return src_field, exchange(True, tgt_counts, lse, pot, first)
 
 
 def solution(mesh):

time: 147 us -> 94.7 us (0.64)
  blocking collectives: 81.3 us -> 0 us
  Pallas kernels: 35.9 us -> 87.1 us
  between operations: 14.1 us -> 0.74 us
  waiting for transfers between devices: 12.3 us -> 0 us
  local copies, waits for them, and re-layouts: 1.24 us -> 6.4 us
  other arithmetic: 1.97 us -> 0 us
    all_gather x3 -> x0, blocking collectives: 81.3 us -> none  [the longest x2 48.9 us: local(): every = lax.all_gather(res[-1], ('loop', 'narrow'))]
    pallas_call x0 -> x3, Pallas kernels: none -> 50.7 us  [the longest x2 33.1 us: exchange(): pl.pallas_call(functools.partial(exchange_kernel, last), out_shape=jax.Sh...]
    all_gather x1 -> x0, waiting for transfers between devices: 11.6 us -> none  [local(): pts = lax.all_gather(tgt_points, 'loop', tiled=True)]
    unnamed x14 -> x23, local copies, waits for them, and re-layouts: 1.24 us -> 6.4 us
  transfers between devices with their start and end apart: 1 -> 0, of which waited for: 1 -> 0; matrix products, arithmetic and copies ran while one was open for 1% -> 0% of each run, Pallas kernels for 0% -> 0%
where the time goes in v2:
time: 94.7 us; the launch traced here: 94.2 us
  Pallas kernels  87.1 us (92%)
  local copies, waits for them, and re-layouts  6.4 us (7%)
    pallas_call x2, Pallas kernels, half_step(): pl.pallas_call(functools.partial(half_step_kernel, final), out_shape=outs...  36.4 us
    pallas_call x2, Pallas kernels, exchange(): pl.pallas_call(functools.partial(exchange_kernel, last), out_shape=jax.Sh...  33.1 us
    pallas_call x1, Pallas kernels, gather(): pl.pallas_call(gather_kernel, out_shape=[jax.ShapeDtypeStruct((targets, f...  17.6 us
    unnamed x23, local copies, waits for them, and re-layouts  6.4 us

profile of v2, /device:TPU:0, one launch (start us, length us, event | category | flops | bytes accessed | tf_op | source)
XLA Modules:
  0.0 94.2 jit_solution(16712096852358986950)
XLA Ops:
  0.6 0.0 copy-start.5
  0.6 0.9 copy-done.5
  1.5 0.0 copy-start.8
  1.5 0.7 copy-done.8
  2.2 17.6 %shard_map.77 = (bf16[64,64,128]{2,1,0:T(8,128)(2,1)S(1)}, f32[64,128]{1,0:T(8,128)S(1)}) custom-call(s32[8]{0:T(128)S(1)} %copy-done.8, bf16[8,64,128]{2,1,0:T(8,128)(2,1)S(1)} %copy-done.5), custom_call_target="tpu_custom_call" | custom-call | tf_op jit(solution)/shard_map/pallas_call | solution.py:241
  19.8 0.0 copy-start.2
  19.8 0.0 copy-start.9
  19.8 0.0 copy-start.10
  19.8 0.0 copy-done.6
  19.8 0.6 copy-done.9
  20.5 0.0 copy-done.10
  20.5 0.9 %copy-done = bf16[16,64,128]{2,1,0:T(8,128)(2,1)S(1)} copy-done((bf16[16,64,128]{2,1,0:T(8,128)(2,1)S(1)}, bf16[16,64,128]{2,1,0:T(8,128)(2,1)}, u32[]{:S(2)}) %copy-start) | copy-done | bytes 262168
  21.5 17.9 %shard_map.78.lse_ref = f32[64,128]{1,0:T(8,128)S(1)} custom-call(s32[16,24]{1,0:T(8,128)S(1)} %copy-done.6, s32[16]{0:T(128)S(1)} %copy-done.9, s32[16]{0:T(128)S(1)} %copy-done.10, bf16[16,64,128]{2,1,0:T(8,128)(2,1)S(1)} %copy-done, bf16[64,64,128]{2,1,0:T(8,128)(2,1)S(1)} %get-tuple-element.6.pts_ref, f32[64,128]{1,0:T(8,128)S(1)} %get-tuple-element.7.pot_ref.refs_0_), custom_call_target="tpu_custom_call" | custom-call | tf_op jit(solution)/shard_map/pallas_call | solution.py:141
  39.4 0.0 copy-done.2
  39.4 0.0 copy-start.4
  39.4 0.6 copy-done.4
  40.0 19.6 %shard_map.79.pot_ref = f32[64,128]{1,0:T(8,128)} custom-call(s32[8]{0:T(128)} %cnt_ref.9, f32[64,128]{1,0:T(8,128)} %copy-done.4, f32[64,128]{1,0:T(8,128)} %copy-done.2), custom_call_target="tpu_custom_call" | custom-call | tf_op jit(solution)/shard_map/pallas_call | solution.py:315
  59.6 0.0 copy-done.1
  59.6 0.0 copy-start.3
  59.6 0.7 copy-done.3
  60.4 18.5 %shard_map.80 = (f32[16,128]{1,0:T(8,128)}, f32[64,128]{1,0:T(8,128)S(1)}) custom-call(s32[16,24]{1,0:T(8,128)S(1)} %copy-done.6, s32[16]{0:T(128)S(1)} %copy-done.9, s32[16]{0:T(128)S(1)} %copy-done.10, bf16[16,64,128]{2,1,0:T(8,128)(2,1)S(1)} %copy-done.1, bf16[64,64,128]{2,1,0:T(8,128)(2,1)S(1)} %get-tuple-element.6.pts_ref, f32[64,128]{1,0:T(8,128)S(1)} %copy-done.3), custom_call_target="tpu_custom_call" | custom-call | tf_op jit(solution)/shard_map/pallas_call | solution.py:141
  78.9 0.6 copy-done.7
  79.5 13.5 %shard_map.81 = f32[8,128]{1,0:T(8,128)} custom-call(s32[8]{0:T(128)} %cnt_ref.9, f32[64,128]{1,0:T(8,128)} %copy-done.7, f32[64,128]{1,0:T(8,128)} %shard_map.79.pot_ref, f32[64,128]{1,0:T(8,128)} %copy-done.2), custom_call_target="tpu_custom_call" | custom-call | tf_op jit(solution)/shard_map/pallas_call | solution.py:315
  93.0 1.3 %copy.9 = f32[8,128]{1,0:T(8,128)} copy(f32[8,128]{1,0:T(8,128)} %shard_map.81) | data formatting | bytes 8192
  (4 shorter events, 0.0 us)
Async XLA Ops:
  0.6 0.9 copy-start.5
  1.5 0.7 copy-start.8
  2.2 17.6 %copy-start.6 = (s32[16,24]{1,0:T(8,128)S(1)}, s32[16,24]{1,0:T(8,128)}, u32[]{:S(2)}) copy-start(s32[16,24]{1,0:T(8,128)} %idx_ref.3) | copy-start | bytes 4612
  19.8 19.6 %copy-start.2 = (f32[64,128]{1,0:T(8,128)}, f32[64,128]{1,0:T(8,128)S(1)}, u32[]{:S(2)}) copy-start(f32[64,128]{1,0:T(8,128)S(1)} %get-tuple-element.7.pot_ref.refs_0_) | copy-start | bytes 98308
  19.8 0.7 copy-start.9
  19.8 0.7 copy-start.10
  20.5 0.9 %copy-start = (bf16[16,64,128]{2,1,0:T(8,128)(2,1)S(1)}, bf16[16,64,128]{2,1,0:T(8,128)(2,1)}, u32[]{:S(2)}) copy-start(bf16[16,64,128]{2,1,0:T(8,128)(2,1)} %src_ref.3) | copy-start | bytes 786436
  21.4 38.2 %copy-start.1 = (bf16[16,64,128]{2,1,0:T(8,128)(2,1)S(1)}, bf16[16,64,128]{2,1,0:T(8,128)(2,1)}, u32[]{:S(2)}) copy-start(bf16[16,64,128]{2,1,0:T(8,128)(2,1)} %src_ref.3) | copy-start | bytes 786436
  39.4 0.6 copy-start.4
  59.6 0.8 copy-start.3
  78.9 0.6 copy-start.7

commit v3 on v2

--- a/solution.py
+++ b/solution.py
@@ -14,7 +14,8 @@
 SCALE = math.log2(math.e) / EPSILON
 DEAD = -1e30
 EMPTY = -1e38
-UNROLL = 4
+WIDE = 8
+NARROW = 4
 STEP = 32
 
 
@@ -22,18 +23,19 @@
     final, idx_ref, len_ref, cnt_ref, src_ref, pts_ref, pot_ref, *refs
 ):
     if final:
-        fld_ref, out_ref, add_ref, sco_ref, peak_ref, sum_ref = refs
+        fld_ref, out_ref, add_ref, left_ref, sco_ref, top_ref, tot_ref, peak_ref, sum_ref = refs
     else:
         fld_ref = None
-        out_ref, add_ref, sco_ref, peak_ref, sum_ref = refs
+        out_ref, add_ref, left_ref, sco_ref, top_ref, tot_ref, peak_ref, sum_ref = refs
     blocks, feat, cells = src_ref.shape
     targets = pot_ref.shape[0]
     f32, bf16 = jnp.float32, jnp.bfloat16
+    depth = feat + 16
 
     rows16 = lax.broadcasted_iota(jnp.int32, (16, cells), 0)
 
     def spread(t, carry):
-        pot = pot_ref[pl.ds(t, 1), :]
+        pot = pot_ref[pl.ds(t, 1), :] * (1.0 / SCALE)
         hi = pot.astype(bf16).astype(f32)
         rest = pot - hi
         mid = rest.astype(bf16).astype(f32)
@@ -47,60 +49,73 @@
     peak_ref[...] = jnp.full(peak_ref.shape, EMPTY, f32)
     sum_ref[...] = jnp.zeros(sum_ref.shape, f32)
 
-    def source_block(i, rows):
+    ones = (lax.broadcasted_iota(jnp.int32, (cells - feat, cells), 0) < 3).astype(f32)
+
+    def turn(i, carry):
+        doubled = src_ref[i].astype(f32) * 2.0
+        left_ref[i] = jnp.concatenate([doubled, ones], axis=0).T.astype(bf16)
+        return carry
+
+    lax.fori_loop(0, blocks, turn, 0, unroll=4)
+
+    def pick(i, k):
         length = len_ref[i]
+        t = idx_ref[i, jnp.minimum(k, length - 1)]
+        return t, jnp.where(k < length, t, targets)
+
+    def score_block(i, rows):
+        left = left_ref[i, :rows, :depth]
+
+        def group(g, carry):
+            peak, total = carry
+            scores = []
+            for u in range(WIDE):
+                k = g * WIDE + u
+                t, ta = pick(i, k)
+                right = jnp.concatenate([pts_ref[t], add_ref[ta]], axis=0)
+                score = jnp.dot(left, right, preferred_element_type=f32) * SCALE
+                sco_ref[i, k, :rows, :] = score
+                scores.append(score)
+            new = peak
+            for score in scores:
+                new = jnp.maximum(new, score)
+            total = total * jnp.exp2(peak - new)
+            for score in scores:
+                total += jnp.exp2(score - new)
+            return new, total
+
+        groups = (len_ref[i] + (WIDE - 1)) // WIDE
+        start = (jnp.full((rows, cells), EMPTY, f32), jnp.zeros((rows, cells), f32))
+        peak, total = lax.fori_loop(0, groups, group, start)
+        top_ref[i, :rows, :] = peak
+        tot_ref[i, :rows, :] = total
+
+    def close_rows(i, carry):
         count = cnt_ref[i]
-        groups = (length + (UNROLL - 1)) // UNROLL
-        source = src_ref[i].astype(f32)
-        scaled = source * (2.0 * SCALE)
-        hi = scaled.astype(bf16).astype(f32)
-        low = scaled - hi
-        both = jnp.concatenate([hi, low], axis=0).T.astype(bf16)[:rows]
-        ones = (lax.broadcasted_iota(jnp.int32, (rows, 16), 1) < 3).astype(f32).astype(bf16)
-        left = jnp.concatenate([both, ones], axis=1)
-
-        def pick(k):
-            live = k < length
-            t = idx_ref[i, jnp.minimum(k, length - 1)]
-            return t, jnp.where(live, t, targets)
-
-        def score_group(g, peak):
-            for u in range(UNROLL):
-                k = g * UNROLL + u
-                t, ta = pick(k)
-                right = jnp.concatenate([pts_ref[t], pts_ref[t], add_ref[ta]], axis=0)
-                score = jnp.dot(left, right, preferred_element_type=f32)
-                sco_ref[k, :rows, :] = score
-                peak = jnp.maximum(peak, score)
-            return peak
-
-        peak = lax.fori_loop(0, groups, score_group, jnp.full((rows, cells), EMPTY, f32))
+        peak = top_ref[i]
         top = jnp.max(peak, axis=1, keepdims=True)
-
-        def row_group(g, total):
-            for u in range(UNROLL):
-                total += jnp.exp2(sco_ref[g * UNROLL + u, :rows, :] - top)
-            return total
-
-        total = lax.fori_loop(0, groups, row_group, jnp.zeros((rows, cells), f32))
-        row_lse = top + jnp.log2(jnp.sum(total, axis=1, keepdims=True))
-        row_iota = lax.broadcasted_iota(jnp.int32, (rows, 1), 0)
-        shift = jnp.where(row_iota < count, -row_lse, DEAD)
-
+        total = jnp.sum(tot_ref[i] * jnp.exp2(peak - top), axis=1, keepdims=True)
+        row_lse = jnp.broadcast_to(top + jnp.log2(total), (cells, cells))
+        sub = lax.broadcasted_iota(jnp.int32, (cells, cells), 0)
+        top_ref[i] = jnp.where(sub < count, -row_lse, DEAD)
         if final:
-            diag = lax.broadcasted_iota(jnp.int32, (rows, cells), 0) == lax.broadcasted_iota(
-                jnp.int32, (rows, cells), 1
+            source = src_ref[i].astype(f32)
+            lane = lax.broadcasted_iota(jnp.int32, (cells, cells), 1)
+            flat = jnp.sum(jnp.where(sub == lane, row_lse, 0.0), axis=0, keepdims=True)
+            squares = jnp.sum(source * source, axis=0, keepdims=True)
+            fld_ref[pl.ds(i, 1), :] = jnp.where(
+                lane[:1] < count, squares - flat * (1.0 / SCALE), 0.0
             )
-            flat = jnp.sum(jnp.where(diag, row_lse, 0.0), axis=0, keepdims=True)
-            squares = jnp.sum(source * source, axis=0, keepdims=True)
-            lane = lax.broadcasted_iota(jnp.int32, (1, cells), 1)
-            fld_ref[pl.ds(i, 1), :] = jnp.where(lane < count, squares - flat * (1.0 / SCALE), 0.0)
-
-        def column_group(g, carry):
-            for u in range(UNROLL):
-                k = g * UNROLL + u
-                _, ta = pick(k)
-                shifted = (sco_ref[k, :rows, :] + shift).reshape(rows // 8, 8, cells)
+        return carry
+
+    def column_block(i, rows):
+        shift = top_ref[i, :rows, :]
+
+        def group(g, carry):
+            for u in range(NARROW):
+                k = g * NARROW + u
+                _, ta = pick(i, k)
+                shifted = (sco_ref[i, k, :rows, :] + shift).reshape(rows // 8, 8, cells)
                 top8 = jnp.max(shifted, axis=0)
                 sum8 = jnp.sum(jnp.exp2(shifted - top8[None]), axis=0)
                 old = peak_ref[ta]
@@ -109,19 +124,20 @@
                 sum_ref[ta] = sum_ref[ta] * jnp.exp2(old - new) + sum8 * jnp.exp2(top8 - new)
             return carry
 
-        lax.fori_loop(0, groups, column_group, 0)
-
-    def each_block(i, carry):
-        steps = (cnt_ref[i] + (STEP - 1)) // STEP
-        for s in range(1, cells // STEP + 1):
-
-            @pl.when(steps == s)
-            def _():
-                source_block(i, s * STEP)
-
-        return carry
-
-    lax.fori_loop(0, blocks, each_block, 0)
+        lax.fori_loop(0, (len_ref[i] + (NARROW - 1)) // NARROW, group, 0)
+
+    def over_blocks(work):
+        def each(i, carry):
+            steps = (cnt_ref[i] + (STEP - 1)) // STEP
+            for s in range(1, cells // STEP + 1):
+                pl.when(steps == s)(functools.partial(work, i, s * STEP))
+            return carry
+
+        lax.fori_loop(0, blocks, each, 0)
+
+    over_blocks(score_block)
+    lax.fori_loop(0, blocks, close_rows, 0, unroll=2)
+    over_blocks(column_block)
 
     peak = peak_ref[:targets]
     top = jnp.max(peak, axis=1, keepdims=True)
@@ -132,7 +148,7 @@
 def half_step(final, block_list, list_len, src_counts, src_points, pts, pot):
     blocks, feat, cells = src_points.shape
     targets = pot.shape[0]
-    slots = -(-block_list.shape[1] // UNROLL) * UNROLL
+    slots = -(-block_list.shape[1] // WIDE) * WIDE
     smem = pl.BlockSpec(memory_space=pltpu.SMEM)
     vmem = pl.BlockSpec(memory_space=pltpu.VMEM)
     outs = [jax.ShapeDtypeStruct((targets, cells), jnp.float32)]
@@ -145,11 +161,14 @@
         out_specs=[vmem] * len(outs),
         scratch_shapes=[
             pltpu.VMEM((targets + 1, 16, cells), jnp.bfloat16),
-            pltpu.VMEM((slots, cells, cells), jnp.float32),
+            pltpu.VMEM((blocks, cells, cells), jnp.bfloat16),
+            pltpu.VMEM((blocks, slots, cells, cells), jnp.float32),
+            pltpu.VMEM((blocks, cells, cells), jnp.float32),
+            pltpu.VMEM((blocks, cells, cells), jnp.float32),
             pltpu.VMEM((targets + 1, 8, cells), jnp.float32),
             pltpu.VMEM((targets + 1, 8, cells), jnp.float32),
         ],
-        compiler_params=pltpu.CompilerParams(vmem_limit_bytes=40 * 1024 * 1024),
+        compiler_params=pltpu.CompilerParams(vmem_limit_bytes=50 * 1024 * 1024),
     )(block_list, list_len, src_counts, src_points, pts, pot)
 
 
@@ -177,7 +196,7 @@
 
 
 def gather_kernel(
-    cnt_ref, tgt_ref, pts_ref, pot_ref,
+    cnt_ref, tgt_ref, pts_ref, pot_ref, live_ref,
     send_sem, recv_sem, pot_send, pot_recv, pass_send, pass_recv, own_sem,
 ):
     me, core = lax.axis_index("loop"), lax.axis_index("narrow")
@@ -201,11 +220,14 @@
     own.start()
 
     lane = lax.broadcasted_iota(jnp.int32, (1, cells), 1)
-    rows = []
+    rows, lives = [], []
     for b in range(blocks):
         cell = tgt_ref[b].astype(jnp.float32)
         square = jnp.sum(cell * cell, axis=0, keepdims=True)
-        rows.append(jnp.where(lane < cnt_ref[b], -SCALE * square, DEAD))
+        live = lane < cnt_ref[b]
+        rows.append(jnp.where(live, -SCALE * square, DEAD))
+        lives.append(jnp.where(live, 1.0, 0.0))
+    live_ref[...] = jnp.concatenate(lives, axis=0)
     mine = pot_ref.at[pl.ds(pl.multiple_of(me * blocks, 8), blocks)]
     mine[...] = jnp.concatenate(rows, axis=0)
     for j, d in enumerate(OFFSETS):
@@ -243,9 +265,10 @@
         out_shape=[
             jax.ShapeDtypeStruct((targets, feat, cells), tgt_points.dtype),
             jax.ShapeDtypeStruct((targets, cells), jnp.float32),
+            jax.ShapeDtypeStruct((blocks, cells), jnp.float32),
         ],
         in_specs=[pl.BlockSpec(memory_space=pltpu.SMEM), vmem],
-        out_specs=[vmem, vmem],
+        out_specs=[vmem, vmem, vmem],
         scratch_shapes=[dma((n,))] * 6 + [dma],
         compiler_params=pltpu.CompilerParams(
             collective_id=0, has_side_effects=True, vmem_limit_bytes=24 * 1024 * 1024
@@ -254,15 +277,14 @@
 
 
 def exchange_kernel(
-    last, cnt_ref, lse_ref, pot_ref, *refs
+    last, live_ref, lse_ref, pot_ref, *refs
 ):
     if last:
         base_ref, out_ref, inbox, send_sem, recv_sem = refs
     else:
         out_ref, inbox, send_sem, recv_sem, pot_send, pot_recv = refs
     me, core = lax.axis_index("loop"), lax.axis_index("narrow")
-    blocks = cnt_ref.shape[0]
-    cells = lse_ref.shape[1]
+    blocks = live_ref.shape[0]
     routes = [(d, side) for d in (0,) + OFFSETS for side in (0, 1) if (d, side) != (0, 0)]
     peers = [{"loop": place(d), "narrow": lax.rem(core + side, 2)} for d, side in routes]
     greet(peers)
@@ -275,12 +297,7 @@
         copy = remote(rows(lse_ref, place(d)), inbox.at[j], send_sem.at[j], recv_sem.at[j], peers[j])
         copy.start()
         sends.append(copy)
-    lane = lax.broadcasted_iota(jnp.int32, (1, cells), 1)
-    lane = jnp.broadcast_to(lane, (blocks, cells))
-    sub = lax.broadcasted_iota(jnp.int32, (blocks, cells), 0)
-    live = lane < cnt_ref[0]
-    for b in range(1, blocks):
-        live = jnp.where(sub == b, (lane < cnt_ref[b]).astype(jnp.int32), live.astype(jnp.int32)) > 0
+    live = live_ref[...] > 0.5
     for j in range(len(routes)):
         sends[j].wait_recv()
     top = own = rows(lse_ref, me)[...]
@@ -306,33 +323,33 @@
         copy.wait_send()
 
 
-def exchange(last, tgt_counts, lse, pot, *base):
+def exchange(last, alive, lse, pot, *base):
     targets, cells = lse.shape
-    blocks = tgt_counts.shape[0]
+    blocks = alive.shape[0]
     vmem = pl.BlockSpec(memory_space=pltpu.VMEM)
     dma = pltpu.SemaphoreType.DMA
     n = 2 * len(OFFSETS) + 1
     return pl.pallas_call(
         functools.partial(exchange_kernel, last),
         out_shape=jax.ShapeDtypeStruct((blocks if last else targets, cells), jnp.float32),
-        in_specs=[pl.BlockSpec(memory_space=pltpu.SMEM)] + [vmem] * (2 + len(base)),
+        in_specs=[vmem] * (3 + len(base)),
         out_specs=vmem,
         scratch_shapes=[pltpu.VMEM((n, blocks, cells), jnp.float32), dma((n,)), dma((n,))]
         + ([] if last else [dma((len(OFFSETS),))] * 2),
         compiler_params=pltpu.CompilerParams(collective_id=2 if last else 1, has_side_effects=True),
-    )(tgt_counts, lse, pot, *base)
+    )(alive, lse, pot, *base)
 
 
 def local(src_points, tgt_points, block_list, list_len, src_counts, tgt_counts):
-    pts, first = gather(tgt_counts, tgt_points)
+    pts, first, alive = gather(tgt_counts, tgt_points)
     listed = (block_list, list_len, src_counts, src_points, pts)
     (lse,) = half_step(False, *listed, first)
-    pot = exchange(False, tgt_counts, lse, first)
+    pot = exchange(False, alive, lse, first)
     for it in range(1, ITERS - 1):
         (lse,) = half_step(False, *listed, pot)
-        pot = exchange(False, tgt_counts, lse, pot)
+        pot = exchange(False, alive, lse, pot)
     src_field, lse = half_step(True, *listed, pot)
-    return src_field, exchange(True, tgt_counts, lse, pot, first)
+    return src_field, exchange(True, alive, lse, pot, first)
 
 
 def solution(mesh):

time: 94.7 us -> 83.4 us (0.88)
  Pallas kernels: 87.1 us -> 74.7 us
    pallas_call x2, Pallas kernels: 33.1 us -> 22.6 us  [exchange(): pl.pallas_call(functools.partial(exchange_kernel, last), out_shape=jax.Sh...]
    pallas_call x2, Pallas kernels: 36.4 us -> 34.5 us  [half_step(): pl.pallas_call(functools.partial(half_step_kernel, final), out_shape=outs...]
    unnamed x23 -> x25, local copies, waits for them, and re-layouts: 6.4 us -> 7 us
where the time goes in v3:
time: 83.4 us; the launch traced here: 82.4 us
  Pallas kernels  74.7 us (90%)
  local copies, waits for them, and re-layouts  7 us (8%)
    pallas_call x2, Pallas kernels, half_step(): pl.pallas_call(functools.partial(half_step_kernel, final), out_shape=outs...  34.5 us
    pallas_call x2, Pallas kernels, exchange(): pl.pallas_call(functools.partial(exchange_kernel, last), out_shape=jax.Sh...  22.6 us
    pallas_call x1, Pallas kernels, gather(): pl.pallas_call(gather_kernel, out_shape=[jax.ShapeDtypeStruct((targets, f...  17.6 us
    unnamed x25, local copies, waits for them, and re-layouts  7 us

profile of v3, /device:TPU:0, one launch (start us, length us, event | category | flops | bytes accessed | tf_op | source)
XLA Modules:
  0.0 82.4 jit_solution(2442175124563485090)
XLA Ops:
  0.6 0.0 copy-start.5
  0.6 0.9 %copy-done.5 = bf16[8,64,128]{2,1,0:T(8,128)(2,1)S(1)} copy-done((bf16[8,64,128]{2,1,0:T(8,128)(2,1)S(1)}, bf16[8,64,128]{2,1,0:T(8,128)(2,1)}, u32[]{:S(2)}) %copy-start.5) | copy-done | bytes 131096
  1.5 0.0 copy-start.11
  1.5 0.7 copy-done.11
  2.2 0.0 copy-start.6
  2.2 17.6 %shard_map.77 = (bf16[64,64,128]{2,1,0:T(8,128)(2,1)S(1)}, f32[64,128]{1,0:T(8,128)S(1)}, f32[8,128]{1,0:T(8,128)S(1)}) custom-call(s32[8]{0:T(128)S(1)} %copy-done.11, bf16[8,64,128]{2,1,0:T(8,128)(2,1)S(1)} %copy-done.5), custom_call_target="tpu_custom_call" | custom-call | tf_op jit(solution)/shard_map/pallas_call | solution.py:263
  19.8 0.0 copy-start.8
  19.8 0.6 copy-done.8
  20.4 0.0 copy-done.6
  20.4 0.7 copy-done.9
  21.1 0.0 copy-done.10
  21.1 0.9 %copy-done = bf16[16,64,128]{2,1,0:T(8,128)(2,1)S(1)} copy-done((bf16[16,64,128]{2,1,0:T(8,128)(2,1)S(1)}, bf16[16,64,128]{2,1,0:T(8,128)(2,1)}, u32[]{:S(2)}) %copy-start) | copy-done | bytes 262168
  22.0 17.0 %shard_map.78.lse_ref = f32[64,128]{1,0:T(8,128)S(1)} custom-call(s32[16,24]{1,0:T(8,128)S(1)} %copy-done.6, s32[16]{0:T(128)S(1)} %copy-done.9, s32[16]{0:T(128)S(1)} %copy-done.10, bf16[16,64,128]{2,1,0:T(8,128)(2,1)S(1)} %copy-done, bf16[64,64,128]{2,1,0:T(8,128)(2,1)S(1)} %get-tuple-element.7.pts_ref, f32[64,128]{1,0:T(8,128)S(1)} %get-tuple-element.9.pot_ref.refs_0_), custom_call_target="tpu_custom_call" | custom-call | tf_op jit(solution)/shard_map/pallas_call | solution.py:157
  39.0 0.0 copy-done.2
  39.0 0.0 copy-start.4
  39.0 0.6 copy-done.4
  39.6 14.4 %shard_map.79.pot_ref = f32[64,128]{1,0:T(8,128)} custom-call(f32[8,128]{1,0:T(8,128)} %copy-done.8, f32[64,128]{1,0:T(8,128)} %copy-done.4, f32[64,128]{1,0:T(8,128)} %copy-done.2), custom_call_target="tpu_custom_call" | custom-call | tf_op jit(solution)/shard_map/pallas_call | solution.py:332
  54.0 0.0 copy-done.1
  54.0 0.0 copy-start.3
  54.1 0.7 copy-done.3
  54.8 17.5 %shard_map.80 = (f32[16,128]{1,0:T(8,128)}, f32[64,128]{1,0:T(8,128)S(1)}) custom-call(s32[16,24]{1,0:T(8,128)S(1)} %copy-done.6, s32[16]{0:T(128)S(1)} %copy-done.9, s32[16]{0:T(128)S(1)} %copy-done.10, bf16[16,64,128]{2,1,0:T(8,128)(2,1)S(1)} %copy-done.1, bf16[64,64,128]{2,1,0:T(8,128)(2,1)S(1)} %get-tuple-element.7.pts_ref, f32[64,128]{1,0:T(8,128)S(1)} %copy-done.3), custom_call_target="tpu_custom_call" | custom-call | tf_op jit(solution)/shard_map/pallas_call | solution.py:157
  72.3 0.6 copy-done.7
  72.9 8.2 %shard_map.81 = f32[8,128]{1,0:T(8,128)} custom-call(f32[8,128]{1,0:T(8,128)} %copy-done.8, f32[64,128]{1,0:T(8,128)} %copy-done.7, f32[64,128]{1,0:T(8,128)} %shard_map.79.pot_ref, f32[64,128]{1,0:T(8,128)} %copy-done.2), custom_call_target="tpu_custom_call" | custom-call | tf_op jit(solution)/shard_map/pallas_call | solution.py:332
  81.1 1.3 %copy.9 = f32[8,128]{1,0:T(8,128)} copy(f32[8,128]{1,0:T(8,128)} %shard_map.81) | data formatting | bytes 8192
  (6 shorter events, 0.0 us)
Async XLA Ops:
  0.6 0.9 %copy-start.5 = (bf16[8,64,128]{2,1,0:T(8,128)(2,1)S(1)}, bf16[8,64,128]{2,1,0:T(8,128)(2,1)}, u32[]{:S(2)}) copy-start(bf16[8,64,128]{2,1,0:T(8,128)(2,1)} %tgt_ref.1) | copy-start | bytes 393220
  1.5 0.7 copy-start.11
  2.2 18.2 %copy-start.6 = (s32[16,24]{1,0:T(8,128)S(1)}, s32[16,24]{1,0:T(8,128)}, u32[]{:S(2)}) copy-start(s32[16,24]{1,0:T(8,128)} %idx_ref.3) | copy-start | bytes 4612
  19.8 0.6 copy-start.8
  20.4 18.6 %copy-start.2 = (f32[64,128]{1,0:T(8,128)}, f32[64,128]{1,0:T(8,128)S(1)}, u32[]{:S(2)}) copy-start(f32[64,128]{1,0:T(8,128)S(1)} %get-tuple-element.9.pot_ref.refs_0_) | copy-start | bytes 98308
  20.4 0.7 copy-start.9
  20.4 0.7 copy-start.10
  21.1 0.9 %copy-start = (bf16[16,64,128]{2,1,0:T(8,128)(2,1)S(1)}, bf16[16,64,128]{2,1,0:T(8,128)(2,1)}, u32[]{:S(2)}) copy-start(bf16[16,64,128]{2,1,0:T(8,128)(2,1)} %src_ref.3) | copy-start | bytes 786436
  22.0 32.0 %copy-start.1 = (bf16[16,64,128]{2,1,0:T(8,128)(2,1)S(1)}, bf16[16,64,128]{2,1,0:T(8,128)(2,1)}, u32[]{:S(2)}) copy-start(bf16[16,64,128]{2,1,0:T(8,128)(2,1)} %src_ref.3) | copy-start | bytes 786436
  39.0 0.6 copy-start.4
  54.0 0.8 copy-start.3
  72.3 0.6 copy-start.7
